TPU v7x, 512 devices: a whole 4x8x8 slice. The times are simulated.
512 devices in a mesh: dp: 16 (over x, y_lo), tensor: 32 (over z, y_hi, core).
Axes of the slice: x: 4, y: 8 (y_hi: 2, y_lo: 4; y = y_hi * 4 + y_lo), z: 8, core: 2. Of those that a mesh axis runs over, the one named last changes fastest.
Arguments:
- out_grad: bfloat16 [12288, 8192], P(('dp', 'tensor')), may hold values from -0.01953125 to 0.01953125
- hidden: bfloat16 [12288, 28672], P('dp', 'tensor'), may hold values from -6 to 6
- projector: bfloat16 [8192, 1024], P('dp'), may hold values from -0.1875 to 0.1875
- moment_one: float32 [1024, 28672], P('dp', 'tensor'), may hold values from -3 to 3
- moment_two: float32 [1024, 28672], P('dp', 'tensor'), may hold values from 0.1 to 2
Outputs:
- update: bfloat16 [28672, 8192], P('tensor', 'dp')
- new_one: float32 [1024, 28672], P('dp', 'tensor')
- new_two: float32 [1024, 28672], P('dp', 'tensor')
All inputs are finite; a program needn't handle non-finite values.
Results may differ from a plain program's by a relative error of at most 0.018.
Values may be sent and summed in bfloat16 or wider, within the bound.
No kernel may reach another device: no remote copies, remote signals or barrier semaphores. Data moves between devices by JAX's collectives and lax.ppermute only.
A program may use at most 64 MiB of HBM per device.

v0:
```python
import jax
import jax.numpy as jnp
from jax import lax
from jax.sharding import PartitionSpec as P

STEP = 1000


def adam_moments(rank_grad, moment_one, moment_two):
    new_one = 0.9 * moment_one + 0.1 * rank_grad
    new_two = 0.999 * moment_two + 0.001 * rank_grad * rank_grad
    first_hat = new_one / (1.0 - 0.9**STEP)
    second_hat = new_two / (1.0 - 0.999**STEP)
    normalized = (first_hat / (jnp.sqrt(second_hat) + 1e-08)).astype(jnp.bfloat16)
    return (normalized, new_one, new_two)


def shards(out_grad, hidden, projector, moment_one, moment_two):
    pieces = lax.all_to_all(out_grad, "dp", split_axis=1, concat_axis=0, tiled=True)
    local_rows = lax.psum_scatter(
        jnp.dot(pieces, projector, preferred_element_type=jnp.float32).astype(jnp.bfloat16),
        "dp",
        scatter_dimension=0,
        tiled=True,
    )
    projected = lax.all_gather(local_rows, "tensor", axis=0, tiled=True)
    own_rows = moment_one.shape[0]
    rank_grad = lax.psum(
        lax.dot_general(
            projected, hidden, (((0,), (0,)), ((), ())), preferred_element_type=jnp.float32
        ).astype(jnp.bfloat16),
        "dp",
    ).astype(jnp.float32)
    all_one, all_two = (
        lax.all_gather(moment_one.astype(jnp.bfloat16), "dp", axis=0, tiled=True).astype(
            moment_one.dtype
        ),
        lax.all_gather(moment_two.astype(jnp.bfloat16), "dp", axis=0, tiled=True).astype(
            moment_two.dtype
        ),
    )
    normalized, full_one, full_two = adam_moments(rank_grad, all_one, all_two)
    offset = lax.axis_index("dp") * own_rows
    new_one = lax.dynamic_slice_in_dim(full_one, offset, own_rows, 0)
    new_two = lax.dynamic_slice_in_dim(full_two, offset, own_rows, 0)
    update = lax.dot_general(
        normalized, projector, (((0,), (1,)), ((), ())), preferred_element_type=jnp.float32
    )
    return (update.astype(jnp.bfloat16), new_one, new_two)


def solution(mesh):
    in_specs = (
        P(("dp", "tensor"), None),
        P("dp", "tensor"),
        P("dp", None),
        P("dp", "tensor"),
        P("dp", "tensor"),
    )
    out_specs = (P("tensor", "dp"), P("dp", "tensor"), P("dp", "tensor"))
    return jax.shard_map(shards, mesh=mesh, in_specs=in_specs, out_specs=out_specs, check_vma=False)
```

profile of v0, /device:TPU:56, one launch (start us, length us, event | category | flops | bytes accessed | tf_op | source)
XLA Modules:
  0.0 576.7 jit_solution(2820782563939885235)
XLA Ops:
  7.2 0.0 copy-start
  7.2 0.0 copy-start.4
  7.2 0.0 copy-start.5
  7.2 0.0 reduce-scatter.2.cloned.1.call-start
  7.2 1.1 copy.12
  8.4 16.4 %all_to_all.19 = bf16[24,16,512]{2,0,1:T(8,128)(2,1)S(1)} all-to-all(bf16[24,16,512]{2,0,1:T(8,128)(2,1)S(1)} %bitcast.12), channel_id=1, replica_groups=mesh['dp'=16,'tensor'=32] {'dp'}, dimensions={1} | all-to-all | bytes 786432 | tf_op jit(solution)/shard_map/all_to_all | solution.py:19
  24.8 2.7 convolution_convert_fusion.1
  27.5 0.0 reduce-scatter.2.cloned.1.call-update
  27.5 0.0 all-gather.6.cloned.1.call-start
  27.6 85.0 %reduce-scatter.2.cloned.1.call-done = bf16[24,1024]{1,0:T(8,128)(2,1)} async-done(((bf16[384,1024]{1,0:T(8,128)(2,1)}), bf16[24,1024]{1,0:T(8,128)(2,1)}) %reduce-scatter.2.cloned.1.call-update) | async-done | bytes 49168 | tf_op jit(solution)/shard_map/reduce_scatter | solution.py:20
  112.5 0.0 all-gather.6.cloned.1.call-update
  112.5 0.0 all-gather.4.cloned.1.call-start
  112.6 0.0 copy-done.4
  112.6 0.7 convert_element_type.27
  113.2 0.0 all-gather.4.cloned.1.call-update
  113.3 0.0 all-gather.8.cloned.1.call-start
  113.3 0.0 copy-done.5
  113.3 0.7 convert_element_type.32
  114.0 0.0 all-gather.8.cloned.1.call-update
  114.0 0.0 all-reduce.2.cloned.1.call-start
  114.1 92.0 %all-gather.6.cloned.1.call-done = bf16[768,1024]{1,0:T(8,128)(2,1)} async-done(((bf16[24,1024]{1,0:T(8,128)(2,1)}), bf16[768,1024]{1,0:T(8,128)(2,1)}) %all-gather.6.cloned.1.call-update) | async-done | bytes 1572880 | tf_op jit(solution)/shard_map/all_gather | solution.py:26
  206.1 0.0 copy-done
  206.1 4.5 convolution_convert_fusion
  210.6 0.0 all-reduce.2.cloned.1.call-update
  210.6 80.0 %all-gather.4.cloned.1.call-done = bf16[1024,896]{1,0:T(8,128)(2,1)} async-done(((bf16[64,896]{1,0:T(8,128)(2,1)}), bf16[1024,896]{1,0:T(8,128)(2,1)}) %all-gather.4.cloned.1.call-update) | async-done | bytes 1835024 | tf_op jit(solution)/shard_map/all_gather | solution.py:35
  290.7 0.0 copy-start.1
  290.7 90.7 %all-gather.8.cloned.1.call-done = bf16[1024,896]{1,0:T(8,128)(2,1)} async-done(((bf16[64,896]{1,0:T(8,128)(2,1)}), bf16[1024,896]{1,0:T(8,128)(2,1)}) %all-gather.8.cloned.1.call-update) | async-done | bytes 1835024 | tf_op jit(solution)/shard_map/all_gather | solution.py:38
  381.4 179.8 %all-reduce.2.cloned.1.call-done = bf16[1024,896]{1,0:T(8,128)(2,1)} async-done(((bf16[1024,896]{1,0:T(8,128)(2,1)}), bf16[1024,896]{1,0:T(8,128)(2,1)}) %all-reduce.2.cloned.1.call-update) | async-done | bytes 1835024 | tf_op jit(solution)/shard_map/psum | solution.py:28
  561.2 0.0 copy-start.2
  561.2 0.0 copy-start.3
  561.2 0.0 copy-start.6
  561.2 3.9 fusion.1
  565.1 0.8 constant_dynamic-slice_fusion
  566.0 0.0 copy-done.1
  566.0 0.0 copy-done.2
  566.0 0.0 copy-done.3
  566.0 0.0 copy-done.6
  566.0 4.2 fusion.3
Async XLA Ops:
  7.2 199.0 %copy-start = (bf16[768,896]{1,0:T(8,128)(2,1)S(1)}, bf16[768,896]{1,0:T(8,128)(2,1)}, u32[]{:S(2)}) copy-start(bf16[768,896]{1,0:T(8,128)(2,1)} %param.6) | copy-start | bytes 4128772
  7.2 105.4 %copy-start.4 = (f32[64,896]{1,0:T(8,128)S(1)}, f32[64,896]{1,0:T(8,128)}, u32[]{:S(2)}) copy-start(f32[64,896]{1,0:T(8,128)} %param.8) | copy-start | bytes 688132
  7.2 106.1 %copy-start.5 = (f32[64,896]{1,0:T(8,128)S(1)}, f32[64,896]{1,0:T(8,128)}, u32[]{:S(2)}) copy-start(f32[64,896]{1,0:T(8,128)} %param.9) | copy-start | bytes 688132
  7.2 105.3 %reduce-scatter.2.cloned.1.call-start = ((), (), s32[]{:S(2)}) async-start(), calls=%async_computation.3 | async-start | bytes 835584 | tf_op jit(solution)/shard_map/reduce_scatter | solution.py:20
  27.5 178.6 %all-gather.6.cloned.1.call-start = ((), (), s32[]{:S(2)}) async-start(), calls=%async_computation.4 | async-start | bytes 1622016 | tf_op jit(solution)/shard_map/all_gather | solution.py:26
  112.5 178.2 %all-gather.4.cloned.1.call-start = ((), (), s32[]{:S(2)}) async-start(), calls=%async_computation.2 | async-start | bytes 1949696 | tf_op jit(solution)/shard_map/all_gather | solution.py:35
  113.3 268.1 %all-gather.8.cloned.1.call-start = ((), (), s32[]{:S(2)}) async-start(), calls=%async_computation.6 | async-start | bytes 1949696 | tf_op jit(solution)/shard_map/all_gather | solution.py:38
  114.0 447.2 %all-reduce.2.cloned.1.call-start = ((), (), s32[]{:S(2)}) async-start(), calls=%async_computation.5 | async-start | bytes 3670016 | tf_op jit(solution)/shard_map/psum | solution.py:28
  290.7 275.3 %copy-start.1 = (bf16[1024,896]{1,0:T(8,128)(2,1)S(1)}, bf16[1024,896]{1,0:T(8,128)(2,1)}, u32[]{:S(2)}) copy-start(bf16[1024,896]{1,0:T(8,128)(2,1)} %all-gather.4.cloned.1.call-done) | copy-start | bytes 5505028
  561.2 4.8 copy-start.2
  561.2 4.8 copy-start.3
  561.2 4.8 copy-start.6
Sparse Core Ops, SparseCore 0:
  27.6 84.8 reduce-scatter.1
  116.4 89.6 all-gather.5
  209.0 81.6 all-gather.3
  293.4 87.9 all-gather.7
  384.5 176.6 all-reduce.1
where the time goes:
time: 583 us; the launch traced here: 577 us
  waiting for transfers between devices  528 us (91%)
  blocking collectives  16.4 us (3%)
  between operations  13.8 us (2%)
  matrix products  11.4 us (2%)
    psum x1, waiting for transfers between devices, shards(): lax.psum(lax.dot_general(projected, hidden, (((0,), (0,)), ((), ())), pre...  180 us
    all_gather x1, waiting for transfers between devices, shards(): projected = lax.all_gather(local_rows, 'tensor', axis=0, tiled=True)  92 us
    all_gather x1, waiting for transfers between devices, shards(): lax.all_gather(moment_two.astype(jnp.bfloat16), 'dp', axis=0, tiled=True)  90.7 us
    reduce_scatter x1, waiting for transfers between devices, shards(): lax.psum_scatter(jnp.dot(pieces, projector, preferred_element_type=jnp.fl...  85 us
    all_gather x1, waiting for transfers between devices, shards(): lax.all_gather(moment_one.astype(jnp.bfloat16), 'dp', axis=0, tiled=True)  80 us
    all_to_all x1, blocking collectives, shards(): lax.all_to_all(out_grad, 'dp', split_axis=1, concat_axis=0, tiled=True)  16.4 us
  transfers between devices with their start and end apart: 5, of which 5 were waited for; matrix products, arithmetic and copies ran while one was open for 1% of the time, Pallas kernels for 0%

commit v1 on v0

v1 whole, which is shorter than its diff:
```python
import jax
import jax.numpy as jnp
from jax import lax
from jax.sharding import Mesh
from jax.sharding import PartitionSpec as P

STEP = 1000

DP = ("x", "yl")
TENSOR = ("z", "yh", "c")


def adam_moments(rank_grad, moment_one, moment_two):
    new_one = 0.9 * moment_one + 0.1 * rank_grad
    new_two = 0.999 * moment_two + 0.001 * rank_grad * rank_grad
    first_hat = new_one / (1.0 - 0.9**STEP)
    second_hat = new_two / (1.0 - 0.999**STEP)
    normalized = (first_hat / (jnp.sqrt(second_hat) + 1e-08)).astype(jnp.bfloat16)
    return (normalized, new_one, new_two)


def exchange(parts, axis):
    return lax.all_to_all(parts, axis, 0, 0)


def summed(parts):
    return jnp.sum(parts.astype(jnp.float32), axis=0)


def shards(out_grad, hidden, projector, moment_one, moment_two):
    n_dp = lax.axis_size(DP)
    n_x, n_yl = lax.axis_size("x"), lax.axis_size("yl")
    n_zy = lax.axis_size(("z", "yh"))
    rows, width = out_grad.shape
    block, rank = projector.shape
    own_rows, columns = moment_one.shape

    pieces = exchange(out_grad.reshape(rows, n_dp, block).swapaxes(0, 1), DP)
    partial = jnp.dot(
        pieces.reshape(n_dp * rows, block), projector, preferred_element_type=jnp.float32
    ).astype(jnp.bfloat16)
    own = summed(exchange(partial.reshape(n_dp, rows, rank), DP)).astype(jnp.bfloat16)

    mine = exchange(jnp.broadcast_to(own, (n_zy, rows, rank)), ("z", "yh"))
    other = lax.ppermute(mine, "c", [(0, 1), (1, 0)])
    core = lax.axis_index("c")
    tokens = hidden.reshape(n_zy, 2, rows, columns)
    group = jnp.zeros((rank, columns), jnp.float32)
    for left, at in ((mine, core), (other, 1 - core)):
        right = lax.dynamic_index_in_dim(tokens, at, 1, keepdims=False)
        group = group + lax.dot_general(
            left.reshape(n_zy * rows, rank),
            right.reshape(n_zy * rows, columns),
            (((0,), (0,)), ((), ())),
            preferred_element_type=jnp.float32,
        )
    group = group.astype(jnp.bfloat16)

    along_x = summed(exchange(group.reshape(n_x, rank // n_x, columns), "x")).astype(jnp.bfloat16)
    rank_grad = summed(exchange(along_x.reshape(n_yl, own_rows, columns), "yl"))

    normalized, new_one, new_two = adam_moments(rank_grad, moment_one, moment_two)

    quarter = exchange(jnp.broadcast_to(normalized, (n_yl, own_rows, columns)), "yl")
    quarter = quarter.reshape(n_yl * own_rows, columns)
    full = exchange(jnp.broadcast_to(quarter, (n_x,) + quarter.shape), "x").reshape(rank, columns)
    update = lax.dot_general(
        full, projector, (((0,), (1,)), ((), ())), preferred_element_type=jnp.float32
    )
    return (update.astype(jnp.bfloat16), new_one, new_two)


def solution(mesh):
    fine = Mesh(mesh.devices.reshape(4, 4, 8, 2, 2), DP + TENSOR)
    in_specs = (
        P(DP + TENSOR, None),
        P(DP, TENSOR),
        P(DP, None),
        P(DP, TENSOR),
        P(DP, TENSOR),
    )
    out_specs = (P(TENSOR, DP), P(DP, TENSOR), P(DP, TENSOR))
    return jax.shard_map(shards, mesh=fine, in_specs=in_specs, out_specs=out_specs, check_vma=False)
```

time: 583 us -> 180 us (0.31)
  waiting for transfers between devices: 528 us -> 0.94 us
  blocking collectives: 16.4 us -> 163 us
  between operations: 13.8 us -> 0.73 us
    all_gather x3 -> x0, waiting for transfers between devices: 263 us -> none  [the longest x1 92 us: shards(): projected = lax.all_gather(local_rows, 'tensor', axis=0, tiled=True)]
    psum x1 -> x0, waiting for transfers between devices: 180 us -> none  [shards(): lax.psum(lax.dot_general(projected, hidden, (((0,), (0,)), ((), ())), pre...]
    all_to_all x1 -> x7, blocking collectives: 16.4 us -> 163 us  [exchange(): return lax.all_to_all(parts, axis, 0, 0)]
    reduce_scatter x1 -> x0, waiting for transfers between devices: 85 us -> none  [shards(): lax.psum_scatter(jnp.dot(pieces, projector, preferred_element_type=jnp.fl...]
  transfers between devices with their start and end apart: 5 -> 1, of which waited for: 5 -> 1; matrix products, arithmetic and copies ran while one was open for 1% -> 1% of each run, Pallas kernels for 0% -> 0%
where the time goes in v1:
time: 180 us; the launch traced here: 177 us
  blocking collectives  163 us (91%)
  matrix products  6.34 us (4%)
  other arithmetic  2.64 us (1%)
  starting transfers between devices  1.91 us (1%)
  local copies, waits for them, and re-layouts  1.88 us (1%)
    all_to_all x7, blocking collectives, exchange(): return lax.all_to_all(parts, axis, 0, 0)  163 us
    dot_general x2, matrix products, shards(): lax.dot_general(left.reshape(n_zy * rows, rank), right.reshape(n_zy * row...  3.65 us
  transfers between devices with their start and end apart: 1, of which 1 were waited for; matrix products, arithmetic and copies ran while one was open for 1% of the time, Pallas kernels for 0%

profile of v1, /device:TPU:56, one launch (start us, length us, event | category | flops | bytes accessed | tf_op | source)
XLA Modules:
  0.0 177.0 jit_solution(1720377712384108026)
XLA Ops:
  0.6 0.0 copy-start
  0.6 1.2 copy.11
  1.9 0.2 copy.10
  2.1 16.4 %all_to_all.35 = bf16[16,24,512]{2,1,0:T(8,128)(2,1)S(1)} all-to-all(bf16[16,24,512]{2,1,0:T(8,128)(2,1)S(1)} %copy.10), channel_id=1, replica_groups=mesh['x'=4,'yl'=4,'z'=8,'yh'=2,'c'=2] {'x','yl'}, dimensions={0} | all-to-all | bytes 786432 | tf_op jit(solution)/shard_map/all_to_all | solution.py:23
  18.5 0.0 copy-done
  18.5 0.6 convolution_convert_fusion.1
  19.1 25.7 %all_to_all.36 = bf16[16,24,1024]{2,1,0:T(8,128)(2,1)S(1)} all-to-all(bf16[16,24,1024]{2,1,0:T(8,128)(2,1)S(1)} %bitcast.32), channel_id=1, replica_groups=mesh['x'=4,'yl'=4,'z'=8,'yh'=2,'c'=2] {'x','yl'}, dimensions={0} | all-to-all | bytes 1572864 | tf_op jit(solution)/shard_map/all_to_all | solution.py:23
  44.8 0.0 copy-start.1
  44.8 0.1 reduce_sum.33
  44.9 0.1 broadcast_in_dim.9
  45.0 36.8 %all_to_all.37 = bf16[16,24,1024]{2,1,0:T(8,128)(2,1)S(1)} all-to-all(bf16[16,24,1024]{2,1,0:T(8,128)(2,1)S(1)} %broadcast_in_dim.9), channel_id=1, replica_groups=mesh['x'=4,'yl'=4,'z'=8,'yh'=2,'c'=2] {'z','yh'}, dimensions={0} | all-to-all | bytes 1572864 | tf_op jit(solution)/shard_map/all_to_all | solution.py:23
  81.8 1.9 %collective-permute-start = (bf16[16,24,1024]{2,1,0:T(8,128)(2,1)S(1)}, bf16[16,24,1024]{2,1,0:T(8,128)(2,1)}, u32[]{:S(2)}, u32[]{:S(2)}) collective-permute-start(bf16[16,24,1024]{2,1,0:T(8,128)(2,1)S(1)} %all_to_all.37), channel_id=1, source_target_pairs={{0,1},{1,0},{2,3},{3,2},{4,5},{5,4},{6,7},{7,6},{8,9},{9,8},{10,11... | collective-permute-start | bytes 2359304 | tf_op jit(solution)/shard_map/ppermute | solution.py:45
  83.7 0.0 copy-done.1
  83.7 0.2 constant_dynamic-slice_fusion
  83.9 1.2 fusion.2
  85.1 0.9 collective-permute-done
  86.1 2.4 %add_convert_fusion = bf16[1024,896]{1,0:T(8,128)(2,1)S(1)} fusion(f32[1024,896]{1,0:T(8,128)S(1)} %fusion.2, bf16[384,1024]{1,0:T(8,128)(2,1)} %bitcast.6, bf16[384,896]{1,0:T(8,128)(2,1)S(1)} %bitcast.25), kind=kOutput, calls=%fused_computation | convolution fusion | flops 706478080 | bytes 6979584 | tf_op jit(solution)/shard_map/dot_general | solution.py:51
  88.5 27.6 %all_to_all.38 = bf16[4,256,896]{2,1,0:T(8,128)(2,1)S(1)} all-to-all(bf16[4,256,896]{2,1,0:T(8,128)(2,1)S(1)} %bitcast.23), channel_id=1, replica_groups=mesh['x'=4,'yl'=4,'z'=8,'yh'=2,'c'=2] {'x'}, dimensions={0} | all-to-all | bytes 3670016 | tf_op jit(solution)/shard_map/all_to_all | solution.py:23
  116.1 0.5 reduce_sum.34
  116.6 15.9 %all_to_all.39 = bf16[4,64,896]{2,1,0:T(8,128)(2,1)S(1)} all-to-all(bf16[4,64,896]{2,1,0:T(8,128)(2,1)S(1)} %bitcast.27), channel_id=1, replica_groups=mesh['x'=4,'yl'=4,'z'=8,'yh'=2,'c'=2] {'yl'}, dimensions={0} | all-to-all | bytes 917504 | tf_op jit(solution)/shard_map/all_to_all | solution.py:23
  132.5 0.1 convert_reduce_fusion
  132.5 2.0 %divide_convert_fusion = (bf16[64,896]{1,0:T(8,128)(2,1)S(1)}, f32[64,896]{1,0:T(8,128)}, f32[64,896]{1,0:T(8,128)}) fusion(f32[64,896]{1,0:T(8,128)S(1)} %convert_reduce_fusion, f32[64,896]{1,0:T(8,128)} %param.9, f32[64,896]{1,0:T(8,128)} %param.8), kind=kLoop, calls=%fused_computation.6 | loop fusion | flops 630784 | bytes 1261568 | tf_op jit(solution)/shard_map/convert_element_type | solution.py:18
  134.5 14.8 %all_to_all.40 = bf16[4,64,896]{2,1,0:T(8,128)(2,1)S(1)} all-to-all(bf16[4,64,896]{2,1,0:T(8,128)(2,1)S(1)} %broadcast_in_dim.10), channel_id=1, replica_groups=mesh['x'=4,'yl'=4,'z'=8,'yh'=2,'c'=2] {'yl'}, dimensions={0} | all-to-all | bytes 917504 | tf_op jit(solution)/shard_map/all_to_all | solution.py:23
  149.4 0.1 broadcast_in_dim.11
  149.5 25.4 %all_to_all.41 = bf16[4,256,896]{2,1,0:T(8,128)(2,1)S(1)} all-to-all(bf16[4,256,896]{2,1,0:T(8,128)(2,1)S(1)} %broadcast_in_dim.11), channel_id=1, replica_groups=mesh['x'=4,'yl'=4,'z'=8,'yh'=2,'c'=2] {'x'}, dimensions={0} | all-to-all | bytes 3670016 | tf_op jit(solution)/shard_map/all_to_all | solution.py:23
  174.9 2.1 %convolution_convert_fusion = bf16[896,512]{1,0:T(8,128)(2,1)} fusion(bf16[1024,896]{1,0:T(8,128)(2,1)S(1)} %bitcast.28, bf16[512,1024]{1,0:T(8,128)(2,1)S(1)} %copy-done), kind=kOutput, calls=%fused_computation.1 | convolution fusion | flops 939982848 | bytes 3801088 | tf_op jit(solution)/shard_map/dot_general | solution.py:67
  (1 shorter events, 0.0 us)
Async XLA Ops:
  0.6 17.9 %copy-start = (bf16[512,1024]{1,0:T(8,128)(2,1)S(1)}, bf16[512,1024]{1,0:T(8,128)(2,1)}, u32[]{:S(2)}) copy-start(bf16[512,1024]{1,0:T(8,128)(2,1)} %param.7) | copy-start | bytes 3145732
  44.8 38.9 %copy-start.1 = (bf16[768,896]{1,0:T(8,128)(2,1)S(1)}, bf16[768,896]{1,0:T(8,128)(2,1)}, u32[]{:S(2)}) copy-start(bf16[768,896]{1,0:T(8,128)(2,1)} %param.6) | copy-start | bytes 4128772
  81.8 4.3 %collective-permute-start = (bf16[16,24,1024]{2,1,0:T(8,128)(2,1)S(1)}, bf16[16,24,1024]{2,1,0:T(8,128)(2,1)}, u32[]{:S(2)}, u32[]{:S(2)}) collective-permute-start(bf16[16,24,1024]{2,1,0:T(8,128)(2,1)S(1)} %all_to_all.37), channel_id=1, source_target_pairs={{0,1},{1,0},{2,3},{3,2},{4,5},{5,4},{6,7},{7,6},{8,9},{9,8},{10,11... | collective-permute-start | bytes 2359304 | tf_op jit(solution)/shard_map/ppermute | solution.py:45

commit v2 on v1

v2 whole, which is shorter than its diff:
```python
import jax
import jax.numpy as jnp
import numpy as np
from jax import lax
from jax.sharding import Mesh
from jax.sharding import PartitionSpec as P

STEP = 1000

DP = ("x", "yl")
TENSOR = ("z", "yh", "c")
SIZES = (4, 4, 8, 2, 2)


def adam_moments(rank_grad, moment_one, moment_two):
    new_one = 0.9 * moment_one + 0.1 * rank_grad
    new_two = 0.999 * moment_two + 0.001 * rank_grad * rank_grad
    first_hat = new_one / (1.0 - 0.9**STEP)
    second_hat = new_two / (1.0 - 0.999**STEP)
    normalized = (first_hat / (jnp.sqrt(second_hat) + 1e-08)).astype(jnp.bfloat16)
    return (normalized, new_one, new_two)


def exchange(parts, axis):
    return lax.all_to_all(parts, axis, 0, 0)


def groups(axes, order):
    names = DP + TENSOR
    ids = np.arange(np.prod(SIZES)).reshape(SIZES)
    inside = [names.index(a) for a in axes]
    outside = [i for i in range(len(names)) if i not in inside]
    size = int(np.prod([SIZES[i] for i in inside]))
    lists = ids.transpose(outside + inside).reshape(-1, 2, size)
    return np.stack([lists[:, 0], lists[:, 1, order]], axis=1).reshape(-1, size).tolist()


def exchange_in(parts, axes, order):
    return lax.all_to_all(
        parts, DP + TENSOR, 0, 0, axis_index_groups=groups(axes, order), tiled=True
    )


def summed(parts):
    return jnp.sum(parts.astype(jnp.float32), axis=0)


def shards(out_grad, hidden, projector, moment_one, moment_two):
    n_dp = lax.axis_size(DP)
    n_x, n_yl = lax.axis_size("x"), lax.axis_size("yl")
    n_zy = lax.axis_size(("z", "yh"))
    rows, width = out_grad.shape
    block, rank = projector.shape
    own_rows, columns = moment_one.shape
    quarter = rank // n_x

    core = lax.axis_index("c")
    tokens = lax.all_gather(hidden, "x", axis=0, tiled=True)

    pieces = exchange(out_grad.reshape(rows, n_dp, block).swapaxes(0, 1), DP)
    partial = jnp.dot(
        pieces.reshape(n_dp * rows, block), projector, preferred_element_type=jnp.float32
    ).astype(jnp.bfloat16)
    partial = partial.reshape(n_x, n_yl, rows, n_x, quarter).transpose(3, 1, 0, 2, 4)
    own = summed(exchange(partial.reshape(n_dp, n_x * rows, quarter), DP)).astype(jnp.bfloat16)

    mine = jnp.broadcast_to(own, (n_zy, n_x * rows, quarter))
    mine = exchange_in(mine, ("z", "yh"), list(range(n_zy))[::-1])
    other = lax.ppermute(mine, "c", [(0, 1), (1, 0)])
    first = lax.axis_index("c") == 0
    both = jnp.stack([jnp.where(first, mine, other), jnp.where(first, other, mine)[::-1]], axis=1)
    left = both.reshape(n_zy, 2, n_x, rows, quarter).transpose(2, 0, 1, 3, 4)
    group = lax.dot_general(
        left.reshape(tokens.shape[0], quarter),
        tokens,
        (((0,), (0,)), ((), ())),
        preferred_element_type=jnp.float32,
    ).astype(jnp.bfloat16)

    blocks = group.reshape(n_yl, own_rows, columns)
    blocks = jnp.where(core == 0, blocks, jnp.roll(blocks, -2, axis=0))
    blocks = exchange_in(blocks, ("yl",), [2, 3, 0, 1])
    rank_grad = summed(blocks)

    normalized, new_one, new_two = adam_moments(rank_grad, moment_one, moment_two)

    part = lax.all_gather(normalized, "yl", axis=0, tiled=True)
    full = exchange(jnp.broadcast_to(part, (n_x,) + part.shape), "x").reshape(rank, columns)
    update = lax.dot_general(
        full, projector, (((0,), (1,)), ((), ())), preferred_element_type=jnp.float32
    )
    return (update.astype(jnp.bfloat16), new_one, new_two)


def solution(mesh):
    fine = Mesh(mesh.devices.reshape(SIZES), DP + TENSOR)
    in_specs = (
        P(DP + TENSOR, None),
        P(DP, TENSOR),
        P(DP, None),
        P(DP, TENSOR),
        P(DP, TENSOR),
    )
    out_specs = (P(TENSOR, DP), P(DP, TENSOR), P(DP, TENSOR))
    return jax.shard_map(shards, mesh=fine, in_specs=in_specs, out_specs=out_specs, check_vma=False)
```

time: 180 us -> 165 us (0.917); the launches traced: 177 us -> 164 us
  blocking collectives: 163 us -> 133 us
  between operations: 0.73 us -> 14.2 us
  waiting for transfers between devices: 0.94 us -> 3.08 us
    all_to_all x7 -> x3, blocking collectives: 163 us -> 64.7 us  [exchange(): return lax.all_to_all(parts, axis, 0, 0)]
    all_to_all x0 -> x2, blocking collectives: none -> 53.3 us  [exchange_in(): lax.all_to_all(parts, DP + TENSOR, 0, 0, axis_index_groups=groups(axes, o...]
    all_gather x0 -> x1, blocking collectives: none -> 15.2 us  [shards(): part = lax.all_gather(normalized, 'yl', axis=0, tiled=True)]
    dot_general x2 -> x1, matrix products: 3.65 us -> 4.38 us  [shards(): lax.dot_general(left.reshape(tokens.shape[0], quarter), tokens, (((0,), (...]
  transfers between devices with their start and end apart: 1 -> 2, of which waited for: 1 -> 1; matrix products, arithmetic and copies ran while one was open for 1% -> 3% of each run, Pallas kernels for 0% -> 0%
where the time goes in v2:
time: 165 us; the launch traced here: 164 us
  blocking collectives  133 us (81%)
  between operations  14.2 us (9%)
  matrix products  7.07 us (4%)
  waiting for transfers between devices  3.08 us (2%)
  other arithmetic  2.55 us (2%)
  local copies, waits for them, and re-layouts  2.48 us (2%)
  starting transfers between devices  1.95 us (1%)
    all_to_all x3, blocking collectives, exchange(): return lax.all_to_all(parts, axis, 0, 0)  64.7 us
    all_to_all x2, blocking collectives, exchange_in(): lax.all_to_all(parts, DP + TENSOR, 0, 0, axis_index_groups=groups(axes, o...  53.3 us
    all_gather x1, blocking collectives, shards(): part = lax.all_gather(normalized, 'yl', axis=0, tiled=True)  15.2 us
    dot_general x1, matrix products, shards(): lax.dot_general(left.reshape(tokens.shape[0], quarter), tokens, (((0,), (...  4.38 us
  transfers between devices with their start and end apart: 2, of which 1 were waited for; matrix products, arithmetic and copies ran while one was open for 3% of the time, Pallas kernels for 0%

profile of v2, /device:TPU:56, one launch (start us, length us, event | category | flops | bytes accessed | tf_op | source)
XLA Modules:
  0.0 164.5 jit_solution(2982582749601263784)
XLA Ops:
  7.2 0.0 copy-start
  7.2 0.0 all-gather.2.cloned.1.call-start
  7.2 0.7 all-gather.2.cloned.1.call-update
  7.9 1.1 copy.15
  9.0 0.2 copy.12
  9.3 16.4 %all_to_all.25 = bf16[16,24,512]{2,1,0:T(8,128)(2,1)S(1)} all-to-all(bf16[16,24,512]{2,1,0:T(8,128)(2,1)S(1)} %copy.12), channel_id=1, replica_groups=mesh['x'=4,'yl'=4,'z'=8,'yh'=2,'c'=2] {'x','yl'}, dimensions={0} | all-to-all | bytes 786432 | tf_op jit(solution)/shard_map/all_to_all | solution.py:25
  25.7 0.0 copy-done
  25.7 0.6 convolution_convert_fusion.1
  26.3 0.6 reshape.36
  26.8 0.1 copy.13
  27.0 25.7 %all_to_all.26 = bf16[16,96,256]{2,1,0:T(8,128)(2,1)S(1)} all-to-all(bf16[16,96,256]{2,1,0:T(8,128)(2,1)S(1)} %bitcast.23), channel_id=1, replica_groups=mesh['x'=4,'yl'=4,'z'=8,'yh'=2,'c'=2] {'x','yl'}, dimensions={0} | all-to-all | bytes 1572864 | tf_op jit(solution)/shard_map/all_to_all | solution.py:25
  52.7 0.1 reduce_sum.21
  52.8 0.1 broadcast_in_dim.6
  52.9 36.5 %all_to_all.27 = bf16[16,96,256]{2,1,0:T(8,128)(2,1)S(1)} all-to-all(bf16[16,96,256]{2,1,0:T(8,128)(2,1)S(1)} %broadcast_in_dim.6), channel_id=1, replica_groups={{0,2,4,6,8,10,12,14,16,18,20,22,24,26,28,30},{31,29,27,25,23,21,19,17,1..., dimensions={0} | all-to-all | bytes 1572864 | tf_op jit(solution)/shard_map/all_to_all | solution.py:39
  89.3 1.9 %collective-permute-start = (bf16[16,96,256]{2,1,0:T(8,128)(2,1)S(1)}, bf16[16,96,256]{2,1,0:T(8,128)(2,1)}, u32[]{:S(2)}, u32[]{:S(2)}) collective-permute-start(bf16[16,96,256]{2,1,0:T(8,128)(2,1)S(1)} %all_to_all.27), channel_id=1, source_target_pairs={{0,1},{1,0},{2,3},{3,2},{4,5},{5,4},{6,7},{7,6},{8,9},{9,8},{10,11... | collective-permute-start | bytes 2359304 | tf_op jit(solution)/shard_map/ppermute | solution.py:69
  91.3 2.4 %collective-permute-done = bf16[16,96,256]{2,1,0:T(8,128)(2,1)} collective-permute-done((bf16[16,96,256]{2,1,0:T(8,128)(2,1)S(1)}, bf16[16,96,256]{2,1,0:T(8,128)(2,1)}, u32[]{:S(2)}, u32[]{:S(2)}) %collective-permute-start) | collective-permute-done | bytes 786464 | tf_op jit(solution)/shard_map/ppermute | solution.py:69
  93.6 1.2 broadcast_select_fusion.1
  94.9 0.1 rev.3
  95.0 0.1 maximum_bitcast_fusion
  95.1 0.1 copy.14
  95.2 0.0 all-gather.2.cloned.1.call-done
  95.3 4.4 %convolution_convert_fusion.2 = bf16[256,896]{1,0:T(8,128)(2,1)S(1)} fusion(bf16[3072,256]{1,0:T(8,128)(2,1)S(1)} %bitcast.28, bf16[3072,896]{1,0:T(8,128)(2,1)} %all-gather.2.cloned.1.call-done), kind=kOutput, calls=%fused_computation.3 | convolution fusion | flops 1409515520 | bytes 7536640 | tf_op jit(solution)/shard_map/dot_general | solution.py:73
  99.7 0.0 copy-start.1
  99.7 0.0 copy-start.2
  99.7 0.1 maximum_select_fusion
  99.8 16.8 %all_to_all.28 = bf16[4,64,896]{2,1,0:T(8,128)(2,1)S(1)} all-to-all(bf16[4,64,896]{2,1,0:T(8,128)(2,1)S(1)} %maximum_select_fusion), channel_id=1, replica_groups={{0,32,64,96},{65,97,1,33},{2,34,66,98},{67,99,3,35},{4,36,68,100},{69,1..., dimensions={0} | all-to-all | bytes 917504 | tf_op jit(solution)/shard_map/all_to_all | solution.py:39
  116.6 0.1 convert_reduce_fusion
  116.7 0.0 copy-done.1
  116.7 0.0 copy-done.2
  116.7 0.9 divide_convert_fusion
  117.6 15.2 %all_gather.7 = bf16[256,896]{1,0:T(8,128)(2,1)S(1)} all-gather(bf16[64,896]{1,0:T(8,128)(2,1)S(1)} %get-tuple-element.3), channel_id=1, replica_groups=mesh['x'=4,'yl'=4,'z'=8,'yh'=2,'c'=2] {'yl'}, dimensions={0}, use_global_device_ids=true | all-gather | bytes 573440 | tf_op jit(solution)/shard_map/all_gather | solution.py:87
  132.8 0.1 broadcast_in_dim.7
  132.9 22.6 %all_to_all.29 = bf16[4,256,896]{2,1,0:T(8,128)(2,1)S(1)} all-to-all(bf16[4,256,896]{2,1,0:T(8,128)(2,1)S(1)} %broadcast_in_dim.7), channel_id=1, replica_groups=mesh['x'=4,'yl'=4,'z'=8,'yh'=2,'c'=2] {'x'}, dimensions={0} | all-to-all | bytes 3670016 | tf_op jit(solution)/shard_map/all_to_all | solution.py:25
  155.5 2.1 %convolution_convert_fusion = bf16[896,512]{1,0:T(8,128)(2,1)} fusion(bf16[1024,896]{1,0:T(8,128)(2,1)S(1)} %bitcast.26, bf16[512,1024]{1,0:T(8,128)(2,1)S(1)} %copy-done), kind=kOutput, calls=%fused_computation.1 | convolution fusion | flops 939982848 | bytes 3801088 | tf_op jit(solution)/shard_map/dot_general | solution.py:89
  (1 shorter events, 0.0 us)
Async XLA Ops:
  7.2 18.5 %copy-start = (bf16[512,1024]{1,0:T(8,128)(2,1)S(1)}, bf16[512,1024]{1,0:T(8,128)(2,1)}, u32[]{:S(2)}) copy-start(bf16[512,1024]{1,0:T(8,128)(2,1)} %param.7) | copy-start | bytes 3145732
  7.2 88.1 %all-gather.2.cloned.1.call-start = ((), (), s32[]{:S(2)}) async-start(), calls=%async_computation.5 | async-start | bytes 6881280 | tf_op jit(solution)/shard_map/all_gather | solution.py:58
  89.3 4.3 %collective-permute-start = (bf16[16,96,256]{2,1,0:T(8,128)(2,1)S(1)}, bf16[16,96,256]{2,1,0:T(8,128)(2,1)}, u32[]{:S(2)}, u32[]{:S(2)}) collective-permute-start(bf16[16,96,256]{2,1,0:T(8,128)(2,1)S(1)} %all_to_all.27), channel_id=1, source_target_pairs={{0,1},{1,0},{2,3},{3,2},{4,5},{5,4},{6,7},{7,6},{8,9},{9,8},{10,11... | collective-permute-start | bytes 2359304 | tf_op jit(solution)/shard_map/ppermute | solution.py:69
  99.7 17.0 %copy-start.1 = (f32[64,896]{1,0:T(8,128)S(1)}, f32[64,896]{1,0:T(8,128)}, u32[]{:S(2)}) copy-start(f32[64,896]{1,0:T(8,128)} %param.9) | copy-start | bytes 688132
  99.7 17.0 %copy-start.2 = (f32[64,896]{1,0:T(8,128)S(1)}, f32[64,896]{1,0:T(8,128)}, u32[]{:S(2)}) copy-start(f32[64,896]{1,0:T(8,128)} %param.8) | copy-start | bytes 688132
Sparse Core Ops, SparseCore 0:
  10.1 76.9 all-gather.1

commit v3 on v2

--- a/solution.py
+++ b/solution.py
@@ -2,6 +2,8 @@
 import jax.numpy as jnp
 import numpy as np
 from jax import lax
+from jax.experimental import pallas as pl
+from jax.experimental.pallas import tpu as pltpu
 from jax.sharding import Mesh
 from jax.sharding import PartitionSpec as P
 
@@ -41,6 +43,70 @@
     )
 
 
+def turn(i):
+    return i // SIZES[1] * SIZES[1] + (i + SIZES[1] // 2) % SIZES[1]
+
+
+def by_block(out_grad, block):
+    rows, width = out_grad.shape
+    n = width // block
+
+    def kernel(in_ref, out_ref, sems):
+        shift = lax.axis_index("c") * (SIZES[1] // 2)
+        copies = []
+        for i in range(n):
+            at = i // SIZES[1] * SIZES[1] + lax.rem(i + shift, SIZES[1])
+            columns = pl.ds(pl.multiple_of(at * block, block), block)
+            copies.append(
+                pltpu.make_async_copy(in_ref.at[:, columns], out_ref.at[i], sems.at[i])
+            )
+        for copy in copies:
+            copy.start()
+        for copy in copies:
+            copy.wait()
+
+    return pl.pallas_call(
+        kernel,
+        in_specs=[pl.BlockSpec(memory_space=pl.ANY)],
+        out_specs=pl.BlockSpec(memory_space=pl.ANY),
+        out_shape=jax.ShapeDtypeStruct((n, rows, block), out_grad.dtype),
+        scratch_shapes=[pltpu.SemaphoreType.DMA((n,))],
+        compiler_params=pltpu.CompilerParams(vmem_limit_bytes=2**20),
+        cost_estimate=pl.CostEstimate(
+            flops=0, bytes_accessed=2 * out_grad.size * out_grad.dtype.itemsize, transcendentals=0
+        ),
+    )(out_grad)
+
+
+def by_core(tokens):
+    n_x, n_zy, n_c, rows, columns = tokens.shape
+
+    def kernel(in_ref, out_ref, sems):
+        copies = [pltpu.make_async_copy(in_ref.at[:, :, 0], out_ref.at[0], sems.at[0])]
+        for i in range(n_zy):
+            copies.append(
+                pltpu.make_async_copy(
+                    in_ref.at[:, n_zy - 1 - i, 1], out_ref.at[1, :, i], sems.at[1 + i]
+                )
+            )
+        for copy in copies:
+            copy.start()
+        for copy in copies:
+            copy.wait()
+
+    return pl.pallas_call(
+        kernel,
+        in_specs=[pl.BlockSpec(memory_space=pl.ANY)],
+        out_specs=pl.BlockSpec(memory_space=pl.ANY),
+        out_shape=jax.ShapeDtypeStruct((n_c, n_x, n_zy, rows, columns), tokens.dtype),
+        scratch_shapes=[pltpu.SemaphoreType.DMA((1 + n_zy,))],
+        compiler_params=pltpu.CompilerParams(vmem_limit_bytes=2**20),
+        cost_estimate=pl.CostEstimate(
+            flops=0, bytes_accessed=2 * tokens.size * tokens.dtype.itemsize, transcendentals=0
+        ),
+    )(tokens)
+
+
 def summed(parts):
     return jnp.sum(parts.astype(jnp.float32), axis=0)
 
@@ -57,25 +123,32 @@
     core = lax.axis_index("c")
     tokens = lax.all_gather(hidden, "x", axis=0, tiled=True)
 
-    pieces = exchange(out_grad.reshape(rows, n_dp, block).swapaxes(0, 1), DP)
+    turned = [turn(i) for i in range(n_dp)]
+
+    pieces = exchange_in(by_block(out_grad, block), DP, turned)
     partial = jnp.dot(
         pieces.reshape(n_dp * rows, block), projector, preferred_element_type=jnp.float32
     ).astype(jnp.bfloat16)
     partial = partial.reshape(n_x, n_yl, rows, n_x, quarter).transpose(3, 1, 0, 2, 4)
-    own = summed(exchange(partial.reshape(n_dp, n_x * rows, quarter), DP)).astype(jnp.bfloat16)
+    partial = partial.reshape(n_dp, n_x * rows, quarter)
+    own = summed(exchange_in(partial, DP, turned)).astype(jnp.bfloat16)
 
     mine = jnp.broadcast_to(own, (n_zy, n_x * rows, quarter))
     mine = exchange_in(mine, ("z", "yh"), list(range(n_zy))[::-1])
+    mine, tokens = lax.optimization_barrier((mine, tokens))
     other = lax.ppermute(mine, "c", [(0, 1), (1, 0)])
-    first = lax.axis_index("c") == 0
-    both = jnp.stack([jnp.where(first, mine, other), jnp.where(first, other, mine)[::-1]], axis=1)
-    left = both.reshape(n_zy, 2, n_x, rows, quarter).transpose(2, 0, 1, 3, 4)
-    group = lax.dot_general(
-        left.reshape(tokens.shape[0], quarter),
-        tokens,
-        (((0,), (0,)), ((), ())),
-        preferred_element_type=jnp.float32,
-    ).astype(jnp.bfloat16)
+    tokens = by_core(tokens.reshape(n_x, n_zy, 2, rows, columns))
+    tokens = tokens.reshape(2, n_x, n_zy * rows, columns)
+    group = jnp.zeros((quarter, columns), jnp.float32)
+    for at, left in ((core, mine), (1 - core, other)):
+        left = left.reshape(n_zy, n_x, rows, quarter).swapaxes(0, 1)
+        group = group + lax.dot_general(
+            left.reshape(n_x, n_zy * rows, quarter),
+            lax.dynamic_index_in_dim(tokens, at, 0, keepdims=False),
+            (((0, 1), (0, 1)), ((), ())),
+            preferred_element_type=jnp.float32,
+        )
+    group = group.astype(jnp.bfloat16)
 
     blocks = group.reshape(n_yl, own_rows, columns)
     blocks = jnp.where(core == 0, blocks, jnp.roll(blocks, -2, axis=0))

time: 165 us -> 162 us (0.982)
  blocking collectives: 133 us -> 130 us
  matrix products: 7.07 us -> 4.7 us
  local copies, waits for them, and re-layouts: 2.48 us -> 4.61 us
    all_to_all x3 -> x1, blocking collectives: 64.7 us -> 22.4 us  [exchange(): return lax.all_to_all(parts, axis, 0, 0)]
    all_to_all x2 -> x4, blocking collectives: 53.3 us -> 92 us  [exchange_in(): lax.all_to_all(parts, DP + TENSOR, 0, 0, axis_index_groups=groups(axes, o...]
    unnamed x7 -> x10, local copies, waits for them, and re-layouts: 1.14 us -> 3.57 us
    ppermute x1, waiting for transfers between devices: 2.38 us -> 0.01 us  [shards(): other = lax.ppermute(mine, 'c', [(0, 1), (1, 0)])]
    dot_general x1 -> x2, matrix products: 4.38 us -> 2.01 us  [shards(): lax.dot_general(left.reshape(n_x, n_zy * rows, quarter), lax.dynamic_inde...]
    all_gather x1, waiting for transfers between devices: 0.02 us -> 1.72 us  [shards(): tokens = lax.all_gather(hidden, 'x', axis=0, tiled=True)]
  transfers between devices with their start and end apart: 2 -> 2, of which waited for: 1 -> 1; matrix products, arithmetic and copies ran while one was open for 3% -> 2% of each run, Pallas kernels for 0% -> 1%
where the time goes in v3:
time: 162 us; the launch traced here: 161 us
  blocking collectives  130 us (80%)
  between operations  14.2 us (9%)
  matrix products  4.7 us (3%)
  local copies, waits for them, and re-layouts  4.61 us (3%)
  waiting for transfers between devices  2.4 us (1%)
  starting transfers between devices  1.95 us (1%)
    all_to_all x4, blocking collectives, exchange_in(): lax.all_to_all(parts, DP + TENSOR, 0, 0, axis_index_groups=groups(axes, o...  92 us
    all_to_all x1, blocking collectives, exchange(): return lax.all_to_all(parts, axis, 0, 0)  22.4 us
    all_gather x1, blocking collectives, shards(): part = lax.all_gather(normalized, 'yl', axis=0, tiled=True)  15.8 us
    unnamed x10, local copies, waits for them, and re-layouts  3.57 us
  transfers between devices with their start and end apart: 2, of which 1 were waited for; matrix products, arithmetic and copies ran while one was open for 2% of the time, Pallas kernels for 1%

profile of v3, /device:TPU:56, one launch (start us, length us, event | category | flops | bytes accessed | tf_op | source)
XLA Modules:
  0.0 160.7 jit_solution(3663587397929014015)
XLA Ops:
  7.2 0.0 copy-start
  7.2 0.0 all-gather.2.cloned.1.call-start
  7.2 0.7 all-gather.2.cloned.1.call-update
  7.9 0.0 copy-start.2
  7.9 1.0 copy-done.2
  8.9 0.4 shard_map.76
  9.3 17.2 %all_to_all.25 = bf16[16,24,512]{2,1,0:T(8,128)(2,1)S(1)} all-to-all(bf16[16,24,512]{2,1,0:T(8,128)(2,1)S(1)} %shard_map.76), channel_id=1, replica_groups={{0,32,64,96,128,160,192,224,256,288,320,352,384,416,448,480},{65,97,1,3..., dimensions={0} | all-to-all | bytes 786432 | tf_op jit(solution)/shard_map/all_to_all | solution.py:41
  26.5 0.0 copy-done
  26.5 0.6 convolution_convert_fusion.1
  27.1 0.6 reshape.42
  27.7 0.1 copy.8
  27.8 24.8 %all_to_all.26 = bf16[16,96,256]{2,1,0:T(8,128)(2,1)S(1)} all-to-all(bf16[16,96,256]{2,1,0:T(8,128)(2,1)S(1)} %bitcast.53), channel_id=1, replica_groups={{0,32,64,96,128,160,192,224,256,288,320,352,384,416,448,480},{65,97,1,3..., dimensions={0} | all-to-all | bytes 1572864 | tf_op jit(solution)/shard_map/all_to_all | solution.py:41
  52.6 0.1 reduce_sum.21
  52.7 0.1 broadcast_in_dim.6
  52.8 32.6 %all_to_all.27 = bf16[16,96,256]{2,1,0:T(8,128)(2,1)S(1)} all-to-all(bf16[16,96,256]{2,1,0:T(8,128)(2,1)S(1)} %broadcast_in_dim.6), channel_id=1, replica_groups={{0,2,4,6,8,10,12,14,16,18,20,22,24,26,28,30},{31,29,27,25,23,21,19,17,1..., dimensions={0} | all-to-all | bytes 1572864 | tf_op jit(solution)/shard_map/all_to_all | solution.py:41
  85.4 1.7 %all-gather.2.cloned.1.call-done = bf16[3072,896]{1,0:T(8,128)(2,1)} async-done(((bf16[768,896]{1,0:T(8,128)(2,1)}), bf16[3072,896]{1,0:T(8,128)(2,1)}) %all-gather.2.cloned.1.call-update) | async-done | bytes 5505040 | tf_op jit(solution)/shard_map/all_gather | solution.py:124
  87.1 1.9 %collective-permute-start = (bf16[16,96,256]{2,1,0:T(8,128)(2,1)S(1)}, bf16[16,96,256]{2,1,0:T(8,128)(2,1)S(1)}, u32[]{:S(2)}, u32[]{:S(2)}) collective-permute-start(bf16[16,96,256]{2,1,0:T(8,128)(2,1)S(1)} %all_to_all.27), channel_id=1, source_target_pairs={{0,1},{1,0},{2,3},{3,2},{4,5},{5,4},{6,7},{7,6},{8,9},{9,8},{10,11... | collective-permute-start | bytes 2359304 | tf_op jit(solution)/shard_map/ppermute | solution.py:139
  89.0 0.0 copy-start.1
  89.0 2.6 %copy-done.1 = bf16[3072,896]{1,0:T(8,128)(2,1)S(1)} copy-done((bf16[3072,896]{1,0:T(8,128)(2,1)S(1)}, bf16[3072,896]{1,0:T(8,128)(2,1)}, u32[]{:S(2)}) %copy-start.1) | copy-done | bytes 5505048
  91.6 1.2 shard_map.77
  92.8 0.1 copy.9
  92.9 1.0 fusion.6
  93.9 0.0 collective-permute-done
  93.9 0.1 copy.11
  93.9 1.0 fusion.15
  95.0 0.0 copy-start.3
  95.0 0.0 copy-start.4
  95.0 0.1 maximum_select_fusion
  95.1 17.4 %all_to_all.28 = bf16[4,64,896]{2,1,0:T(8,128)(2,1)S(1)} all-to-all(bf16[4,64,896]{2,1,0:T(8,128)(2,1)S(1)} %maximum_select_fusion), channel_id=1, replica_groups={{0,32,64,96},{65,97,1,33},{2,34,66,98},{67,99,3,35},{4,36,68,100},{69,1..., dimensions={0} | all-to-all | bytes 917504 | tf_op jit(solution)/shard_map/all_to_all | solution.py:41
  112.5 0.1 convert_reduce_fusion
  112.5 0.0 copy-done.3
  112.5 0.0 copy-done.4
  112.5 0.9 divide_convert_fusion
  113.4 15.8 %all_gather.7 = bf16[256,896]{1,0:T(8,128)(2,1)S(1)} all-gather(bf16[64,896]{1,0:T(8,128)(2,1)S(1)} %get-tuple-element.7), channel_id=1, replica_groups=mesh['x'=4,'yl'=4,'z'=8,'yh'=2,'c'=2] {'yl'}, dimensions={0}, use_global_device_ids=true | all-gather | bytes 573440 | tf_op jit(solution)/shard_map/all_gather | solution.py:160
  129.2 0.1 broadcast_in_dim.7
  129.4 22.4 %all_to_all.29 = bf16[4,256,896]{2,1,0:T(8,128)(2,1)S(1)} all-to-all(bf16[4,256,896]{2,1,0:T(8,128)(2,1)S(1)} %broadcast_in_dim.7), channel_id=1, replica_groups=mesh['x'=4,'yl'=4,'z'=8,'yh'=2,'c'=2] {'x'}, dimensions={0} | all-to-all | bytes 3670016 | tf_op jit(solution)/shard_map/all_to_all | solution.py:27
  151.7 2.1 %convolution_convert_fusion = bf16[896,512]{1,0:T(8,128)(2,1)} fusion(bf16[1024,896]{1,0:T(8,128)(2,1)S(1)} %bitcast.54, bf16[512,1024]{1,0:T(8,128)(2,1)S(1)} %copy-done), kind=kOutput, calls=%fused_computation.6 | convolution fusion | flops 939982848 | bytes 3801088 | tf_op jit(solution)/shard_map/dot_general | solution.py:162
  (1 shorter events, 0.0 us)
Async XLA Ops:
  7.2 19.4 %copy-start = (bf16[512,1024]{1,0:T(8,128)(2,1)S(1)}, bf16[512,1024]{1,0:T(8,128)(2,1)}, u32[]{:S(2)}) copy-start(bf16[512,1024]{1,0:T(8,128)(2,1)} %param.7) | copy-start | bytes 3145732
  7.2 79.9 %all-gather.2.cloned.1.call-start = ((), (), s32[]{:S(2)}) async-start(), calls=%async_computation.5 | async-start | bytes 6881280 | tf_op jit(solution)/shard_map/all_gather | solution.py:124
  7.9 1.0 copy-start.2
  87.1 6.8 %collective-permute-start = (bf16[16,96,256]{2,1,0:T(8,128)(2,1)S(1)}, bf16[16,96,256]{2,1,0:T(8,128)(2,1)S(1)}, u32[]{:S(2)}, u32[]{:S(2)}) collective-permute-start(bf16[16,96,256]{2,1,0:T(8,128)(2,1)S(1)} %all_to_all.27), channel_id=1, source_target_pairs={{0,1},{1,0},{2,3},{3,2},{4,5},{5,4},{6,7},{7,6},{8,9},{9,8},{10,11... | collective-permute-start | bytes 2359304 | tf_op jit(solution)/shard_map/ppermute | solution.py:139
  89.0 2.6 %copy-start.1 = (bf16[3072,896]{1,0:T(8,128)(2,1)S(1)}, bf16[3072,896]{1,0:T(8,128)(2,1)}, u32[]{:S(2)}) copy-start(bf16[3072,896]{1,0:T(8,128)(2,1)} %all-gather.2.cloned.1.call-done) | copy-start | bytes 16515076
  95.0 17.6 %copy-start.3 = (f32[64,896]{1,0:T(8,128)S(1)}, f32[64,896]{1,0:T(8,128)}, u32[]{:S(2)}) copy-start(f32[64,896]{1,0:T(8,128)} %param.9) | copy-start | bytes 688132
  95.0 17.6 %copy-start.4 = (f32[64,896]{1,0:T(8,128)S(1)}, f32[64,896]{1,0:T(8,128)}, u32[]{:S(2)}) copy-start(f32[64,896]{1,0:T(8,128)} %param.8) | copy-start | bytes 688132
Sparse Core Ops, SparseCore 0:
  10.1 76.9 all-gather.1

commit v4 on v2

--- a/solution.py
+++ b/solution.py
@@ -2,6 +2,8 @@
 import jax.numpy as jnp
 import numpy as np
 from jax import lax
+from jax.experimental import pallas as pl
+from jax.experimental.pallas import tpu as pltpu
 from jax.sharding import Mesh
 from jax.sharding import PartitionSpec as P
 
@@ -10,6 +12,7 @@
 DP = ("x", "yl")
 TENSOR = ("z", "yh", "c")
 SIZES = (4, 4, 8, 2, 2)
+BY_YH = [z * SIZES[3] + yh for yh in range(SIZES[3]) for z in range(SIZES[2])]
 
 
 def adam_moments(rank_grad, moment_one, moment_two):
@@ -25,20 +28,78 @@
     return lax.all_to_all(parts, axis, 0, 0)
 
 
-def groups(axes, order):
+def groups(axes, first, second):
     names = DP + TENSOR
     ids = np.arange(np.prod(SIZES)).reshape(SIZES)
     inside = [names.index(a) for a in axes]
     outside = [i for i in range(len(names)) if i not in inside]
     size = int(np.prod([SIZES[i] for i in inside]))
     lists = ids.transpose(outside + inside).reshape(-1, 2, size)
-    return np.stack([lists[:, 0], lists[:, 1, order]], axis=1).reshape(-1, size).tolist()
+    return np.stack([lists[:, 0, first], lists[:, 1, second]], axis=1).reshape(-1, size).tolist()
 
 
-def exchange_in(parts, axes, order):
+def exchange_in(parts, axes, second, first=None):
+    first = list(range(len(second))) if first is None else first
     return lax.all_to_all(
-        parts, DP + TENSOR, 0, 0, axis_index_groups=groups(axes, order), tiled=True
+        parts, DP + TENSOR, 0, 0, axis_index_groups=groups(axes, first, second), tiled=True
     )
+
+
+def turn(i):
+    return i // SIZES[1] * SIZES[1] + (i + SIZES[1] // 2) % SIZES[1]
+
+
+def ordered(out_grad, hidden, block):
+    rows, width = out_grad.shape
+    n = width // block
+    n_zy, n_c = hidden.shape[:2]
+
+    def kernel(out_grad_ref, hidden_ref, blocks_ref, tokens_ref, blocks, tokens, sems, out_sems):
+        shift = lax.axis_index("c") * (SIZES[1] // 2)
+        reads = []
+        for i in range(n):
+            at = i // SIZES[1] * SIZES[1] + lax.rem(i + shift, SIZES[1])
+            columns = pl.ds(pl.multiple_of(at * block, block), block)
+            reads.append((out_grad_ref.at[:, columns], blocks.at[i]))
+        for i in range(n_zy):
+            reads.append((hidden_ref.at[BY_YH[i], 0], tokens.at[0, i]))
+        for i in range(n_zy):
+            reads.append((hidden_ref.at[BY_YH[n_zy - 1 - i], 1], tokens.at[1, i]))
+        reads = [pltpu.make_async_copy(*pair, sems.at[i]) for i, pair in enumerate(reads)]
+        writes = [
+            pltpu.make_async_copy(here, there, out_sems.at[i])
+            for i, (here, there) in enumerate(
+                ((blocks, blocks_ref), (tokens.at[0], tokens_ref.at[0]), (tokens.at[1], tokens_ref.at[1]))
+            )
+        ]
+        for read in reads:
+            read.start()
+        for part, write in zip((reads[:n], reads[n : n + n_zy], reads[n + n_zy :]), writes):
+            for read in part:
+                read.wait()
+            write.start()
+        for write in writes:
+            write.wait()
+
+    whole = pl.BlockSpec(memory_space=pl.ANY)
+    return pl.pallas_call(
+        kernel,
+        in_specs=[whole, whole],
+        out_specs=[whole, whole],
+        out_shape=[
+            jax.ShapeDtypeStruct((n, rows, block), out_grad.dtype),
+            jax.ShapeDtypeStruct((n_c, n_zy) + hidden.shape[2:], hidden.dtype),
+        ],
+        scratch_shapes=[
+            pltpu.VMEM((n, rows, block), out_grad.dtype),
+            pltpu.VMEM((n_c, n_zy) + hidden.shape[2:], hidden.dtype),
+            pltpu.SemaphoreType.DMA((n + 2 * n_zy,)),
+            pltpu.SemaphoreType.DMA((3,)),
+        ],
+        cost_estimate=pl.CostEstimate(
+            flops=0, bytes_accessed=4 * (out_grad.size + hidden.size), transcendentals=0
+        ),
+    )(out_grad, hidden)
 
 
 def summed(parts):
@@ -55,27 +116,35 @@
     quarter = rank // n_x
 
     core = lax.axis_index("c")
-    tokens = lax.all_gather(hidden, "x", axis=0, tiled=True)
+    pieces, tokens = ordered(out_grad, hidden.reshape(n_zy, 2, rows, columns), block)
 
-    pieces = exchange(out_grad.reshape(rows, n_dp, block).swapaxes(0, 1), DP)
+    tokens = lax.all_gather(tokens.reshape(-1, columns), "x", axis=0, tiled=True)
+
+    turned = [turn(i) for i in range(n_dp)]
+
+    pieces = exchange_in(pieces, DP, turned)
     partial = jnp.dot(
         pieces.reshape(n_dp * rows, block), projector, preferred_element_type=jnp.float32
     ).astype(jnp.bfloat16)
     partial = partial.reshape(n_x, n_yl, rows, n_x, quarter).transpose(3, 1, 0, 2, 4)
-    own = summed(exchange(partial.reshape(n_dp, n_x * rows, quarter), DP)).astype(jnp.bfloat16)
+    partial = partial.reshape(n_dp, n_x * rows, quarter)
+    own = summed(exchange_in(partial, DP, turned)).astype(jnp.bfloat16)
 
     mine = jnp.broadcast_to(own, (n_zy, n_x * rows, quarter))
-    mine = exchange_in(mine, ("z", "yh"), list(range(n_zy))[::-1])
+    mine = exchange_in(mine, ("z", "yh"), BY_YH[::-1], BY_YH)
+    mine, tokens = lax.optimization_barrier((mine, tokens))
     other = lax.ppermute(mine, "c", [(0, 1), (1, 0)])
-    first = lax.axis_index("c") == 0
-    both = jnp.stack([jnp.where(first, mine, other), jnp.where(first, other, mine)[::-1]], axis=1)
-    left = both.reshape(n_zy, 2, n_x, rows, quarter).transpose(2, 0, 1, 3, 4)
-    group = lax.dot_general(
-        left.reshape(tokens.shape[0], quarter),
-        tokens,
-        (((0,), (0,)), ((), ())),
-        preferred_element_type=jnp.float32,
-    ).astype(jnp.bfloat16)
+    tokens = tokens.reshape(n_x, 2, n_zy * rows, columns)
+    group = jnp.zeros((quarter, columns), jnp.float32)
+    for at, left in ((core, mine), (1 - core, other)):
+        left = left.reshape(n_zy, n_x, rows, quarter).swapaxes(0, 1)
+        group = group + lax.dot_general(
+            left.reshape(n_x, n_zy * rows, quarter),
+            lax.dynamic_index_in_dim(tokens, at, 1, keepdims=False),
+            (((0, 1), (0, 1)), ((), ())),
+            preferred_element_type=jnp.float32,
+        )
+    group = group.astype(jnp.bfloat16)
 
     blocks = group.reshape(n_yl, own_rows, columns)
     blocks = jnp.where(core == 0, blocks, jnp.roll(blocks, -2, axis=0))

time: 165 us -> 161 us (0.976)
  blocking collectives: 133 us -> 130 us
  Pallas kernels: 0 us -> 2.83 us
  waiting for transfers between devices: 3.08 us -> 1.39 us
    all_to_all x3 -> x1, blocking collectives: 64.7 us -> 22.9 us  [exchange(): return lax.all_to_all(parts, axis, 0, 0)]
    all_to_all x2 -> x4, blocking collectives: 53.3 us -> 91.5 us  [exchange_in(): lax.all_to_all(parts, DP + TENSOR, 0, 0, axis_index_groups=groups(axes, f...]
    pallas_call x0 -> x1, Pallas kernels: none -> 2.83 us  [ordered(): pl.pallas_call(kernel, in_specs=[whole, whole], out_specs=[whole, whole],...]
    ppermute x1, waiting for transfers between devices: 2.38 us -> 0.01 us  [shards(): other = lax.ppermute(mine, 'c', [(0, 1), (1, 0)])]
    dot_general x1 -> x2, matrix products: 4.38 us -> 3.96 us  [shards(): lax.dot_general(left.reshape(n_x, n_zy * rows, quarter), lax.dynamic_inde...]
where the time goes in v4:
time: 161 us; the launch traced here: 160 us
  blocking collectives  130 us (81%)
  between operations  14.2 us (9%)
  matrix products  6.64 us (4%)
  Pallas kernels  2.83 us (2%)
  starting transfers between devices  1.95 us (1%)
    all_to_all x4, blocking collectives, exchange_in(): lax.all_to_all(parts, DP + TENSOR, 0, 0, axis_index_groups=groups(axes, f...  91.5 us
    all_to_all x1, blocking collectives, exchange(): return lax.all_to_all(parts, axis, 0, 0)  22.9 us
    all_gather x1, blocking collectives, shards(): part = lax.all_gather(normalized, 'yl', axis=0, tiled=True)  15.8 us
    dot_general x2, matrix products, shards(): lax.dot_general(left.reshape(n_x, n_zy * rows, quarter), lax.dynamic_inde...  3.96 us
  transfers between devices with their start and end apart: 2, of which 1 were waited for; matrix products, arithmetic and copies ran while one was open for 3% of the time, Pallas kernels for 0%

profile of v4, /device:TPU:56, one launch (start us, length us, event | category | flops | bytes accessed | tf_op | source)
XLA Modules:
  0.0 159.7 jit_solution(3789511705338180919)
XLA Ops:
  7.2 0.0 copy-start
  7.2 0.0 all-gather.2.cloned.1.call-start
  7.2 2.8 %shard_map.76 = (bf16[16,24,512]{2,1,0:T(8,128)(2,1)}, bf16[2,16,24,896]{3,2,1,0:T(8,128)(2,1)}) custom-call(bf16[24,8192]{1,0:T(8,128)(2,1)} %out_grad_ref.1, bf16[16,2,24,896]{3,2,1,0:T(8,128)(2,1)} %bitcast.59), custom_call_target="tpu_custom_call" | custom-call | bytes 3538944 | tf_op jit(solution)/shard_map/pallas_call | solution.py:85
  10.1 0.0 all-gather.2.cloned.1.call-update
  10.1 17.4 %all_to_all.25 = bf16[16,24,512]{2,1,0:T(8,128)(2,1)S(1)} all-to-all(bf16[16,24,512]{2,1,0:T(8,128)(2,1)} %get-tuple-element.7), channel_id=1, replica_groups={{0,32,64,96,128,160,192,224,256,288,320,352,384,416,448,480},{65,97,1,3..., dimensions={0} | all-to-all | bytes 786432 | tf_op jit(solution)/shard_map/all_to_all | solution.py:43
  27.5 0.0 copy-done
  27.5 0.6 convolution_convert_fusion.1
  28.1 0.6 reshape.46
  28.7 0.1 copy.10
  28.8 24.8 %all_to_all.26 = bf16[16,96,256]{2,1,0:T(8,128)(2,1)S(1)} all-to-all(bf16[16,96,256]{2,1,0:T(8,128)(2,1)S(1)} %bitcast.57), channel_id=1, replica_groups={{0,32,64,96,128,160,192,224,256,288,320,352,384,416,448,480},{65,97,1,3..., dimensions={0} | all-to-all | bytes 1572864 | tf_op jit(solution)/shard_map/all_to_all | solution.py:43
  53.6 0.1 reduce_sum.21
  53.7 0.1 broadcast_in_dim.6
  53.8 32.0 %all_to_all.27 = bf16[16,96,256]{2,1,0:T(8,128)(2,1)S(1)} all-to-all(bf16[16,96,256]{2,1,0:T(8,128)(2,1)S(1)} %broadcast_in_dim.6), channel_id=1, replica_groups={{0,4,8,12,16,20,24,28,2,6,10,14,18,22,26,30},{31,27,23,19,15,11,7,3,29,..., dimensions={0} | all-to-all | bytes 1572864 | tf_op jit(solution)/shard_map/all_to_all | solution.py:43
  85.8 1.4 all-gather.2.cloned.1.call-done
  87.2 1.9 %collective-permute-start = (bf16[16,96,256]{2,1,0:T(8,128)(2,1)S(1)}, bf16[16,96,256]{2,1,0:T(8,128)(2,1)S(1)}, u32[]{:S(2)}, u32[]{:S(2)}) collective-permute-start(bf16[16,96,256]{2,1,0:T(8,128)(2,1)S(1)} %all_to_all.27), channel_id=1, source_target_pairs={{0,1},{1,0},{2,3},{3,2},{4,5},{5,4},{6,7},{7,6},{8,9},{9,8},{10,11... | collective-permute-start | bytes 2359304 | tf_op jit(solution)/shard_map/ppermute | solution.py:136
  89.1 0.1 copy.11
  89.2 0.0 copy-start.1
  89.2 3.0 %fusion.6 = f32[256,896]{1,0:T(8,128)S(1)} fusion(bf16[4,384,256]{2,1,0:T(8,128)(2,1)S(1)} %bitcast.53, bf16[4,2,384,896]{3,2,1,0:T(8,128)(2,1)} %bitcast.51, s32[]{:T(128)S(6)} %select_n.16), kind=kOutput, calls=%fused_computation.8 | convolution fusion | flops 704643072 | bytes 4456452 | tf_op jit(solution)/shard_map/dot_general | solution.py:141
  92.1 0.0 collective-permute-done
  92.1 0.1 copy.14
  92.2 0.4 copy-done.1
  92.6 1.0 fusion.15
  93.6 0.0 copy-start.2
  93.6 0.0 copy-start.3
  93.6 0.1 maximum_select_fusion
  93.7 17.2 %all_to_all.28 = bf16[4,64,896]{2,1,0:T(8,128)(2,1)S(1)} all-to-all(bf16[4,64,896]{2,1,0:T(8,128)(2,1)S(1)} %maximum_select_fusion), channel_id=1, replica_groups={{0,32,64,96},{65,97,1,33},{2,34,66,98},{67,99,3,35},{4,36,68,100},{69,1..., dimensions={0} | all-to-all | bytes 917504 | tf_op jit(solution)/shard_map/all_to_all | solution.py:43
  110.9 0.1 convert_reduce_fusion
  111.0 0.0 copy-done.2
  111.0 0.0 copy-done.3
  111.0 0.9 divide_convert_fusion
  111.9 15.8 %all_gather.7 = bf16[256,896]{1,0:T(8,128)(2,1)S(1)} all-gather(bf16[64,896]{1,0:T(8,128)(2,1)S(1)} %get-tuple-element.11), channel_id=1, replica_groups=mesh['x'=4,'yl'=4,'z'=8,'yh'=2,'c'=2] {'yl'}, dimensions={0}, use_global_device_ids=true | all-gather | bytes 573440 | tf_op jit(solution)/shard_map/all_gather | solution.py:156
  127.7 0.1 broadcast_in_dim.7
  127.8 22.9 %all_to_all.29 = bf16[4,256,896]{2,1,0:T(8,128)(2,1)S(1)} all-to-all(bf16[4,256,896]{2,1,0:T(8,128)(2,1)S(1)} %broadcast_in_dim.7), channel_id=1, replica_groups=mesh['x'=4,'yl'=4,'z'=8,'yh'=2,'c'=2] {'x'}, dimensions={0} | all-to-all | bytes 3670016 | tf_op jit(solution)/shard_map/all_to_all | solution.py:28
  150.7 2.1 %convolution_convert_fusion = bf16[896,512]{1,0:T(8,128)(2,1)} fusion(bf16[1024,896]{1,0:T(8,128)(2,1)S(1)} %bitcast.58, bf16[512,1024]{1,0:T(8,128)(2,1)S(1)} %copy-done), kind=kOutput, calls=%fused_computation.6 | convolution fusion | flops 939982848 | bytes 3801088 | tf_op jit(solution)/shard_map/dot_general | solution.py:158
  (1 shorter events, 0.0 us)
Async XLA Ops:
  7.2 20.4 %copy-start = (bf16[512,1024]{1,0:T(8,128)(2,1)S(1)}, bf16[512,1024]{1,0:T(8,128)(2,1)}, u32[]{:S(2)}) copy-start(bf16[512,1024]{1,0:T(8,128)(2,1)} %param.7) | copy-start | bytes 3145732
  7.2 80.0 %all-gather.2.cloned.1.call-start = ((), (), s32[]{:S(2)}) async-start(), calls=%async_computation.5 | async-start | bytes 6881280 | tf_op jit(solution)/shard_map/all_gather | solution.py:121
  87.2 5.0 %collective-permute-start = (bf16[16,96,256]{2,1,0:T(8,128)(2,1)S(1)}, bf16[16,96,256]{2,1,0:T(8,128)(2,1)S(1)}, u32[]{:S(2)}, u32[]{:S(2)}) collective-permute-start(bf16[16,96,256]{2,1,0:T(8,128)(2,1)S(1)} %all_to_all.27), channel_id=1, source_target_pairs={{0,1},{1,0},{2,3},{3,2},{4,5},{5,4},{6,7},{7,6},{8,9},{9,8},{10,11... | collective-permute-start | bytes 2359304 | tf_op jit(solution)/shard_map/ppermute | solution.py:136
  89.2 3.4 %copy-start.1 = (bf16[3072,896]{1,0:T(8,128)(2,1)S(1)}, bf16[3072,896]{1,0:T(8,128)(2,1)}, u32[]{:S(2)}) copy-start(bf16[3072,896]{1,0:T(8,128)(2,1)} %all-gather.2.cloned.1.call-done) | copy-start | bytes 16515076
  93.6 17.5 %copy-start.2 = (f32[64,896]{1,0:T(8,128)S(1)}, f32[64,896]{1,0:T(8,128)}, u32[]{:S(2)}) copy-start(f32[64,896]{1,0:T(8,128)} %param.9) | copy-start | bytes 688132
  93.6 17.5 %copy-start.3 = (f32[64,896]{1,0:T(8,128)S(1)}, f32[64,896]{1,0:T(8,128)}, u32[]{:S(2)}) copy-start(f32[64,896]{1,0:T(8,128)} %param.8) | copy-start | bytes 688132
Sparse Core Ops, SparseCore 0:
  10.2 76.9 all-gather.1

commit v5 on v4

--- a/solution.py
+++ b/solution.py
@@ -57,24 +57,24 @@
     def kernel(out_grad_ref, hidden_ref, blocks_ref, tokens_ref, blocks, tokens, sems, out_sems):
         shift = lax.axis_index("c") * (SIZES[1] // 2)
         reads = []
+        for i in range(n_zy):
+            reads.append((hidden_ref.at[BY_YH[i], 0], tokens.at[0, i]))
+        for i in range(n_zy):
+            reads.append((hidden_ref.at[BY_YH[n_zy - 1 - i], 1], tokens.at[1, i]))
         for i in range(n):
             at = i // SIZES[1] * SIZES[1] + lax.rem(i + shift, SIZES[1])
             columns = pl.ds(pl.multiple_of(at * block, block), block)
             reads.append((out_grad_ref.at[:, columns], blocks.at[i]))
-        for i in range(n_zy):
-            reads.append((hidden_ref.at[BY_YH[i], 0], tokens.at[0, i]))
-        for i in range(n_zy):
-            reads.append((hidden_ref.at[BY_YH[n_zy - 1 - i], 1], tokens.at[1, i]))
         reads = [pltpu.make_async_copy(*pair, sems.at[i]) for i, pair in enumerate(reads)]
         writes = [
             pltpu.make_async_copy(here, there, out_sems.at[i])
             for i, (here, there) in enumerate(
-                ((blocks, blocks_ref), (tokens.at[0], tokens_ref.at[0]), (tokens.at[1], tokens_ref.at[1]))
+                ((tokens.at[0], tokens_ref.at[0]), (tokens.at[1], tokens_ref.at[1]), (blocks, blocks_ref))
             )
         ]
         for read in reads:
             read.start()
-        for part, write in zip((reads[:n], reads[n : n + n_zy], reads[n + n_zy :]), writes):
+        for part, write in zip((reads[:n_zy], reads[n_zy : 2 * n_zy], reads[2 * n_zy :]), writes):
             for read in part:
                 read.wait()
             write.start()
@@ -123,10 +123,14 @@
     turned = [turn(i) for i in range(n_dp)]
 
     pieces = exchange_in(pieces, DP, turned)
-    partial = jnp.dot(
-        pieces.reshape(n_dp * rows, block), projector, preferred_element_type=jnp.float32
-    ).astype(jnp.bfloat16)
-    partial = partial.reshape(n_x, n_yl, rows, n_x, quarter).transpose(3, 1, 0, 2, 4)
+    pieces = pieces.reshape(n_dp * rows, block)
+    partial = [
+        jnp.dot(
+            pieces, projector[:, i * quarter : (i + 1) * quarter], preferred_element_type=jnp.float32
+        ).astype(jnp.bfloat16)
+        for i in range(n_x)
+    ]
+    partial = jnp.stack(partial).reshape(n_x, n_x, n_yl, rows, quarter).swapaxes(1, 2)
     partial = partial.reshape(n_dp, n_x * rows, quarter)
     own = summed(exchange_in(partial, DP, turned)).astype(jnp.bfloat16)
 

time: 161 us -> 161 us (level)
  no operation moved by 1% of the time
where the time goes in v5:
time: 161 us; the launch traced here: 160 us
  blocking collectives  130 us (81%)
  between operations  14.2 us (9%)
  matrix products  7.16 us (4%)
  Pallas kernels  2.81 us (2%)
  starting transfers between devices  1.95 us (1%)
    all_to_all x4, blocking collectives, exchange_in(): lax.all_to_all(parts, DP + TENSOR, 0, 0, axis_index_groups=groups(axes, f...  91.4 us
    all_to_all x1, blocking collectives, exchange(): return lax.all_to_all(parts, axis, 0, 0)  22.9 us
    all_gather x1, blocking collectives, shards(): part = lax.all_gather(normalized, 'yl', axis=0, tiled=True)  15.8 us
    dot_general x2, matrix products, shards(): lax.dot_general(left.reshape(n_x, n_zy * rows, quarter), lax.dynamic_inde...  3.95 us
  transfers between devices with their start and end apart: 2, of which 1 were waited for; matrix products, arithmetic and copies ran while one was open for 3% of the time, Pallas kernels for 0%

profile of v5, /device:TPU:56, one launch (start us, length us, event | category | flops | bytes accessed | tf_op | source)
XLA Modules:
  0.0 159.6 jit_solution(2122580648229305042)
XLA Ops:
  7.2 0.0 copy-start.3
  7.2 0.0 all-gather.2.cloned.1.call-start
  7.2 2.8 %shard_map.76 = (bf16[16,24,512]{2,1,0:T(8,128)(2,1)}, bf16[2,16,24,896]{3,2,1,0:T(8,128)(2,1)}) custom-call(bf16[24,8192]{1,0:T(8,128)(2,1)} %out_grad_ref.1, bf16[16,2,24,896]{3,2,1,0:T(8,128)(2,1)} %bitcast.65), custom_call_target="tpu_custom_call" | custom-call | bytes 3538944 | tf_op jit(solution)/shard_map/pallas_call | solution.py:85
  10.0 0.0 all-gather.2.cloned.1.call-update
  10.1 17.4 %all_to_all.25 = bf16[16,24,512]{2,1,0:T(8,128)(2,1)S(1)} all-to-all(bf16[16,24,512]{2,1,0:T(8,128)(2,1)} %get-tuple-element.7), channel_id=1, replica_groups={{0,32,64,96,128,160,192,224,256,288,320,352,384,416,448,480},{65,97,1,3..., dimensions={0} | all-to-all | bytes 786432 | tf_op jit(solution)/shard_map/all_to_all | solution.py:43
  27.5 0.0 copy-done.3
  27.5 0.3 convolution_convert_fusion.4
  27.8 0.3 convolution_convert_fusion.3
  28.1 0.3 convolution_convert_fusion.2
  28.4 0.3 convolution_convert_fusion.1
  28.6 0.1 pad_maximum_fusion
  28.8 0.1 copy.22
  28.8 24.8 %all_to_all.26 = bf16[16,96,256]{2,1,0:T(8,128)(2,1)S(1)} all-to-all(bf16[16,96,256]{2,1,0:T(8,128)(2,1)S(1)} %bitcast.63), channel_id=1, replica_groups={{0,32,64,96,128,160,192,224,256,288,320,352,384,416,448,480},{65,97,1,3..., dimensions={0} | all-to-all | bytes 1572864 | tf_op jit(solution)/shard_map/all_to_all | solution.py:43
  53.6 0.1 reduce_sum.21
  53.7 0.1 broadcast_in_dim.6
  53.8 32.0 %all_to_all.27 = bf16[16,96,256]{2,1,0:T(8,128)(2,1)S(1)} all-to-all(bf16[16,96,256]{2,1,0:T(8,128)(2,1)S(1)} %broadcast_in_dim.6), channel_id=1, replica_groups={{0,4,8,12,16,20,24,28,2,6,10,14,18,22,26,30},{31,27,23,19,15,11,7,3,29,..., dimensions={0} | all-to-all | bytes 1572864 | tf_op jit(solution)/shard_map/all_to_all | solution.py:43
  85.8 1.4 all-gather.2.cloned.1.call-done
  87.2 1.9 %collective-permute-start = (bf16[16,96,256]{2,1,0:T(8,128)(2,1)S(1)}, bf16[16,96,256]{2,1,0:T(8,128)(2,1)S(1)}, u32[]{:S(2)}, u32[]{:S(2)}) collective-permute-start(bf16[16,96,256]{2,1,0:T(8,128)(2,1)S(1)} %all_to_all.27), channel_id=1, source_target_pairs={{0,1},{1,0},{2,3},{3,2},{4,5},{5,4},{6,7},{7,6},{8,9},{9,8},{10,11... | collective-permute-start | bytes 2359304 | tf_op jit(solution)/shard_map/ppermute | solution.py:140
  89.1 0.1 copy.14
  89.2 0.0 copy-start
  89.2 2.9 %fusion.6 = f32[256,896]{1,0:T(8,128)S(1)} fusion(bf16[4,384,256]{2,1,0:T(8,128)(2,1)S(1)} %bitcast.59, bf16[4,2,384,896]{3,2,1,0:T(8,128)(2,1)} %bitcast.57, s32[]{:T(128)S(6)} %select_n.16), kind=kOutput, calls=%fused_computation.7 | convolution fusion | flops 704643072 | bytes 4456452 | tf_op jit(solution)/shard_map/dot_general | solution.py:145
  92.2 0.0 collective-permute-done
  92.2 0.1 copy.17
  92.2 0.4 copy-done
  92.6 1.0 fusion.15
  93.6 0.0 copy-start.1
  93.6 0.0 copy-start.2
  93.7 0.1 maximum_select_fusion
  93.7 17.2 %all_to_all.28 = bf16[4,64,896]{2,1,0:T(8,128)(2,1)S(1)} all-to-all(bf16[4,64,896]{2,1,0:T(8,128)(2,1)S(1)} %maximum_select_fusion), channel_id=1, replica_groups={{0,32,64,96},{65,97,1,33},{2,34,66,98},{67,99,3,35},{4,36,68,100},{69,1..., dimensions={0} | all-to-all | bytes 917504 | tf_op jit(solution)/shard_map/all_to_all | solution.py:43
  110.9 0.1 convert_reduce_fusion
  111.0 0.0 copy-done.1
  111.0 0.0 copy-done.2
  111.0 0.9 divide_convert_fusion
  111.9 15.8 %all_gather.7 = bf16[256,896]{1,0:T(8,128)(2,1)S(1)} all-gather(bf16[64,896]{1,0:T(8,128)(2,1)S(1)} %get-tuple-element.11), channel_id=1, replica_groups=mesh['x'=4,'yl'=4,'z'=8,'yh'=2,'c'=2] {'yl'}, dimensions={0}, use_global_device_ids=true | all-gather | bytes 573440 | tf_op jit(solution)/shard_map/all_gather | solution.py:160
  127.7 0.1 broadcast_in_dim.7
  127.8 22.9 %all_to_all.29 = bf16[4,256,896]{2,1,0:T(8,128)(2,1)S(1)} all-to-all(bf16[4,256,896]{2,1,0:T(8,128)(2,1)S(1)} %broadcast_in_dim.7), channel_id=1, replica_groups=mesh['x'=4,'yl'=4,'z'=8,'yh'=2,'c'=2] {'x'}, dimensions={0} | all-to-all | bytes 3670016 | tf_op jit(solution)/shard_map/all_to_all | solution.py:28
  150.7 2.1 %convolution_convert_fusion = bf16[896,512]{1,0:T(8,128)(2,1)} fusion(bf16[1024,896]{1,0:T(8,128)(2,1)S(1)} %bitcast.64, bf16[512,1024]{1,0:T(8,128)(2,1)S(1)} %copy-done.3), kind=kOutput, calls=%fused_computation.6 | convolution fusion | flops 939982848 | bytes 3801088 | tf_op jit(solution)/shard_map/dot_general | solution.py:162
  (1 shorter events, 0.0 us)
Async XLA Ops:
  7.2 20.3 %copy-start.3 = (bf16[512,1024]{1,0:T(8,128)(2,1)S(1)}, bf16[512,1024]{1,0:T(8,128)(2,1)}, u32[]{:S(2)}) copy-start(bf16[512,1024]{1,0:T(8,128)(2,1)} %param.7) | copy-start | bytes 3145732
  7.2 80.0 %all-gather.2.cloned.1.call-start = ((), (), s32[]{:S(2)}) async-start(), calls=%async_computation.5 | async-start | bytes 6881280 | tf_op jit(solution)/shard_map/all_gather | solution.py:121
  87.2 5.0 %collective-permute-start = (bf16[16,96,256]{2,1,0:T(8,128)(2,1)S(1)}, bf16[16,96,256]{2,1,0:T(8,128)(2,1)S(1)}, u32[]{:S(2)}, u32[]{:S(2)}) collective-permute-start(bf16[16,96,256]{2,1,0:T(8,128)(2,1)S(1)} %all_to_all.27), channel_id=1, source_target_pairs={{0,1},{1,0},{2,3},{3,2},{4,5},{5,4},{6,7},{7,6},{8,9},{9,8},{10,11... | collective-permute-start | bytes 2359304 | tf_op jit(solution)/shard_map/ppermute | solution.py:140
  89.2 3.4 %copy-start = (bf16[3072,896]{1,0:T(8,128)(2,1)S(1)}, bf16[3072,896]{1,0:T(8,128)(2,1)}, u32[]{:S(2)}) copy-start(bf16[3072,896]{1,0:T(8,128)(2,1)} %all-gather.2.cloned.1.call-done) | copy-start | bytes 16515076
  93.6 17.4 %copy-start.1 = (f32[64,896]{1,0:T(8,128)S(1)}, f32[64,896]{1,0:T(8,128)}, u32[]{:S(2)}) copy-start(f32[64,896]{1,0:T(8,128)} %param.9) | copy-start | bytes 688132
  93.6 17.4 %copy-start.2 = (f32[64,896]{1,0:T(8,128)S(1)}, f32[64,896]{1,0:T(8,128)}, u32[]{:S(2)}) copy-start(f32[64,896]{1,0:T(8,128)} %param.8) | copy-start | bytes 688132
Sparse Core Ops, SparseCore 0:
  10.2 76.9 all-gather.1
